TPU v7x, 32 devices: a whole 2x2x4 slice. The times are simulated.
32 devices in a mesh: groups: 2 (over y), freq: 4 (over z), src: 2 (over x), vp: 2 (over core).
Axes of the slice: x: 2, y: 2, z: 4, core: 2. Of those that a mesh axis runs over, the one named last changes fastest.
Arguments:
- first_field: float32 [64, 1536, 512], P(('groups', 'src', 'vp'), 'freq'), parts along dimension 0, may hold values from -6 to 6
- onset: int32 [64, 1536], P(('groups', 'src', 'vp'), 'freq'), parts along dimension 0, may hold values from 64 to 447
- kernel: float32 [56, 2, 1536, 1536], P(('groups', 'freq'), None, 'src'), parts along dimension 0, may hold values from -0.4375 to 0.4375
- bin_owner: int32 [24], replicated, may hold values from 0 to 3, as said below
Outputs:
- focusing: float32 [64, 1536, 512], P(('groups', 'src', 'vp'), 'freq'), parts along dimension 0
There are 2 independent parts, one for each index of `groups`. A program takes and returns all parts, laid end to end along the dimension named above; an argument that names none is the same for every part. Nothing has to cross between parts.
Inputs may be any that keep to these rules, and one draw needn't show every extreme that they name: bin_owner never falls; no freq index owns more than 7 bins and one owns exactly 7; the bins of freq index d sit in increasing order in its first slots of kernel, slots d * 7 on.
All inputs are finite; a program needn't handle non-finite values.
Results may differ from a plain program's by a relative error of at most 0.0001.
Values sent between devices are 32-bit elements; how exact they have to be, the bound alone decides.
No kernel may reach another device: no remote copies, remote signals or barrier semaphores. Data moves between devices by JAX's collectives and lax.ppermute only.
A program may use at most 448 MiB of HBM per device.

v0:
```python
import math

import jax
import jax.numpy as jnp
from jax import lax
from jax.sharding import PartitionSpec as P

NT = 512
NF = 24
FIRST_BIN = 4
ITERS = 2


highest_precision = lax.Precision.HIGHEST


def slot_tables(bin_owner, slots_here, total_slots):
    bin_index = jnp.arange(NF, dtype=jnp.int32)
    earlier = (bin_owner[:, None] == bin_owner[None, :]) & (bin_index[None, :] < bin_index[:, None])
    rank = jnp.sum(earlier.astype(jnp.int32), axis=1)
    slot_of = bin_owner * slots_here + rank
    onehot = (slot_of[:, None] == jnp.arange(total_slots, dtype=jnp.int32)[None, :]).astype(
        jnp.float32
    )
    sample = jnp.arange(NT, dtype=jnp.int32)
    phase = sample[:, None] * (FIRST_BIN + bin_index)[None, :] % NT
    angle = phase.astype(jnp.float32) * (2.0 * math.pi / NT)
    cosine = jnp.dot(jnp.cos(angle), onehot, precision=highest_precision)
    sine = jnp.dot(jnp.sin(angle), onehot, precision=highest_precision)
    scale = 2.0 / NT
    forward_table = jnp.stack([cosine, -sine], axis=2).reshape(NT, 2 * total_slots)
    inverse_table = jnp.stack([cosine.T * scale, -(sine.T * scale)], axis=1).reshape(
        2 * total_slots, NT
    )
    return (forward_table, inverse_table)


def convolve_pairs(spectrum, kernel_view):

    def product(left, right):
        return jnp.einsum("edcvr,cfsdr->efcvs", left, right, precision=highest_precision)

    real_out = product(spectrum[:, :, :, 0], kernel_view[:, 0]) - product(
        spectrum[:, :, :, 1], kernel_view[:, 1]
    )
    imag_out = product(spectrum[:, :, :, 1], kernel_view[:, 0]) + product(
        spectrum[:, :, :, 0], kernel_view[:, 1]
    )
    return jnp.stack([real_out, imag_out], axis=3)


def correlate_pairs(spectrum, kernel_view):

    def product(left, right):
        return jnp.einsum("efcvr,cfrdq->edcvq", left, right, precision=highest_precision)

    real_out = product(spectrum[:, :, :, 0], kernel_view[:, 0]) + product(
        spectrum[:, :, :, 1], kernel_view[:, 1]
    )
    imag_out = product(spectrum[:, :, :, 1], kernel_view[:, 0]) - product(
        spectrum[:, :, :, 0], kernel_view[:, 1]
    )
    return jnp.stack([real_out, imag_out], axis=3)


def local(first_field, onset, kernel, bin_owner):
    slots_here = kernel.shape[0]
    freq_count = lax.axis_size("freq")
    src_count = lax.axis_size("src")
    sub_blocks = freq_count // src_count
    total_slots = slots_here * freq_count
    forward_table, inverse_table = slot_tables(bin_owner, slots_here, total_slots)
    points = first_field.shape[0]
    traces = first_field.shape[1]
    kernel_view = kernel.reshape(slots_here, 2, sub_blocks, traces, freq_count, traces)
    sample = jnp.arange(NT, dtype=jnp.int32)
    keep = (sample[None, None, :] < onset[:, :, None]).astype(jnp.float32)

    def to_bins(field):
        spectrum = jnp.einsum("vrt,tc->cvr", field, forward_table, precision=highest_precision)
        spectrum = spectrum.reshape(freq_count, slots_here, 2, points, traces)
        return lax.all_to_all(spectrum, "freq", split_axis=0, concat_axis=0, tiled=True)

    def to_time(spectrum):
        regrouped = lax.all_to_all(spectrum, "freq", split_axis=0, concat_axis=0, tiled=True)
        flat = regrouped.reshape(2 * total_slots, points, traces)
        return jnp.einsum("cvr,ct->vrt", flat, inverse_table, precision=highest_precision)

    def widen(spectrum):
        return lax.all_gather(spectrum[None], "src", axis=0, tiled=True)

    focusing = first_field
    for sweep in range(ITERS):
        widened = widen(to_bins(focusing))
        direct = convolve_pairs(widened, kernel_view)
        direct = lax.all_to_all(direct, "src", split_axis=0, concat_axis=0, tiled=True)
        direct = direct.reshape(freq_count, slots_here, 2, points, traces)
        down = keep * to_time(direct)
        spectrum = to_bins(down)
        local_part = lax.dynamic_slice_in_dim(
            widen(spectrum), lax.axis_index("src") * sub_blocks, sub_blocks, 1
        )
        partial_terms = correlate_pairs(local_part, kernel_view)
        summed = lax.psum_scatter(partial_terms, "src", scatter_dimension=0, tiled=True)
        summed = summed.reshape(freq_count, slots_here, 2, points, traces)
        focusing = first_field + keep * to_time(summed)
    return focusing


def solution(mesh):
    in_specs = (
        P(("groups", "src", "vp"), "freq", None),
        P(("groups", "src", "vp"), "freq"),
        P(("groups", "freq"), None, "src", None),
        P(),
    )
    out_specs = P(("groups", "src", "vp"), "freq", None)
    return jax.shard_map(local, mesh=mesh, in_specs=in_specs, out_specs=out_specs, check_vma=False)
```

profile of v0, /device:TPU:0, one launch (start us, length us, event | category | flops | bytes accessed | tf_op | source)
XLA Modules:
  0.0 1033.8 jit_solution(6191951822907662321)
XLA Ops:
  10.9 8.6 fusion.46
  20.5 6.3 all-to-all-start
  27.1 74.3 %reshape.50 = f32[7,2,2,384,4,384]{5,4,3,2,1,0:T(4,128)} reshape(f32[7,2,768,1536]{3,2,1,0:T(8,128)} %param.6) | data formatting | bytes 132120576 | tf_op jit(solution)/shard_map/reshape | solution.py:75
  102.2 44.7 %fusion.199 = (f32[7,1,2,384,4,384]{5,4,3,2,1,0:T(4,128)}, f32[7,1,2,384,4,384]{5,4,3,2,1,0:T(4,128)}) fusion(f32[7,2,2,384,4,384]{5,4,3,2,1,0:T(4,128)} %reshape.50), kind=kLoop, calls=%fused_computation.164 | loop fusion | bytes 132120576 | tf_op jit(solution)/shard_map/slice | solution.py:44
  146.9 1.5 copy.85
  148.4 34.1 %fusion.109 = f32[7,2,8,2,384]{4,2,3,1,0:T(8,128)S(1)} fusion(f32[7,1,2,384,4,384]{5,4,3,2,1,0:T(4,128)} %get-tuple-element.6, f32[2,4,7,2,8,384]{5,4,1,0,2,3:T(8,128)S(1)} %bitcast.327), kind=kOutput, calls=%fused_computation.81 | convolution fusion | flops 1585446912 | bytes 34062336 | tf_op jit(solution)/shard_map/edcvr,cfsdr->efcvs/dot_general | solution.py:41
  182.5 34.6 %fusion.106 = f32[7,2,8,2,384]{4,2,3,1,0:T(8,128)S(1)} fusion(f32[7,1,2,384,4,384]{5,4,3,2,1,0:T(4,128)} %get-tuple-element.6, f32[2,4,7,2,8,384]{5,4,1,0,2,3:T(8,128)S(1)} %bitcast.328), kind=kOutput, calls=%fused_computation.80 | convolution fusion | flops 1585446912 | bytes 34062336 | tf_op jit(solution)/shard_map/edcvr,cfsdr->efcvs/dot_general | solution.py:41
  217.1 34.4 %fusion.145 = f32[2,2,7,1,8,384]{5,4,1,0,2,3:T(8,128)S(1)} fusion(f32[7,2,8,2,384]{4,2,3,1,0:T(8,128)S(1)} %fusion.109, f32[7,1,2,384,4,384]{5,4,3,2,1,0:T(4,128)} %get-tuple-element.5, f32[2,4,7,2,8,384]{5,4,1,0,2,3:T(8,128)S(1)} %bitcast.329), kind=kOutput, calls=%fused_computation.93 | convolution fusion | flops 1585532928 | bytes 34406400 | tf_op jit(solution)/shard_map/edcvr,cfsdr->efcvs/dot_general | solution.py:41
  251.5 34.4 %fusion.151 = f32[2,2,7,1,8,384]{5,4,1,0,2,3:T(8,128)S(1)} fusion(f32[7,2,8,2,384]{4,2,3,1,0:T(8,128)S(1)} %fusion.106, f32[7,1,2,384,4,384]{5,4,3,2,1,0:T(4,128)} %get-tuple-element.5, f32[2,4,7,2,8,384]{5,4,1,0,2,3:T(8,128)S(1)} %bitcast.330), kind=kOutput, calls=%fused_computation.95 | convolution fusion | flops 1585532928 | bytes 34406400 | tf_op jit(solution)/shard_map/edcvr,cfsdr->efcvs/dot_general | solution.py:41
  286.1 12.3 %all_to_all.50 = f32[2,2,7,2,8,384]{5,4,1,2,3,0:T(8,128)S(1)} all-to-all(f32[2,2,7,2,8,384]{5,4,1,2,3,0:T(8,128)S(1)} %copy.88), channel_id=1, replica_groups=mesh['groups'=2,'freq'=4,'src'=2,'vp'=2] {'src'}, dimensions={0} | all-to-all | bytes 1376256 | tf_op jit(solution)/shard_map/all_to_all | solution.py:96
  299.3 4.0 all-to-all-start.2
  303.8 16.3 %all-to-all-done.2 = f32[4,7,2,8,384]{4,3,2,1,0:T(8,128)S(1)} async-done(((f32[4,7,2,8,384]{4,3,2,1,0:T(8,128)}), f32[4,7,2,8,384]{4,3,2,1,0:T(8,128)S(1)}, u32[]{:S(2)}, u32[]{:S(2)}) %all-to-all-start.2) | async-done | bytes 688160 | tf_op jit(solution)/shard_map/all_to_all | solution.py:85
  320.1 5.2 fusion.159
  325.3 7.0 fusion.44
  332.4 20.6 %all_to_all.51 = f32[4,7,2,8,384]{4,3,2,1,0:T(8,128)} all-to-all(f32[4,7,2,8,384]{4,3,2,1,0:T(8,128)S(1)} %copy.93), channel_id=1, replica_groups=mesh['groups'=2,'freq'=4,'src'=2,'vp'=2] {'freq'}, dimensions={0} | all-to-all | bytes 1376256 | tf_op jit(solution)/shard_map/all_to_all | solution.py:82
  353.5 24.0 %all-gather.11.cloned.1.call-done = f32[8,7,2,8,384]{4,3,2,1,0:T(8,128)} async-done(((f32[4,7,2,8,384]{4,3,2,1,0:T(8,128)}), f32[8,7,2,8,384]{4,3,2,1,0:T(8,128)}) %all-gather.11.cloned.1.call-update) | async-done | bytes 1376272 | tf_op jit(solution)/shard_map/all_gather | solution.py:90
  377.5 1.5 copy.94
  379.0 25.2 %fusion.58 = f32[7,2,8,4,384]{4,2,3,1,0:T(8,128)S(1)} fusion(f32[2,4,7,2,8,384]{5,4,1,0,2,3:T(8,128)S(1)} %bitcast.339, s32[]{:T(128)S(6)} %select_n.14, f32[7,1,2,384,4,384]{5,4,3,2,1,0:T(4,128)} %get-tuple-element.6), kind=kOutput, calls=%fused_computation.64 | convolution fusion | flops 1585446912 | bytes 34062340 | tf_op jit(solution)/shard_map/efcvr,cfrdq->edcvq/dot_general | solution.py:55
  404.1 25.3 %fusion.61 = f32[7,2,8,4,384]{4,2,3,1,0:T(8,128)S(1)} fusion(f32[2,4,7,2,8,384]{5,4,1,0,2,3:T(8,128)S(1)} %bitcast.340, s32[]{:T(128)S(6)} %select_n.14, s32[]{:T(128)S(6)} %add.76, f32[7,1,2,384,4,384]{5,4,3,2,1,0:T(4,128)} %get-tuple-element.6), kind=kOutput, calls=%fused_computation.65 | convolution fusion | flops 1585446912 | bytes 34062344 | tf_op jit(solution)/shard_map/efcvr,cfrdq->edcvq/dot_general | solution.py:55
  429.4 25.4 %fusion.97 = f32[2,4,7,1,8,384]{5,4,1,0,2,3:T(8,128)S(1)} fusion(f32[7,2,8,4,384]{4,2,3,1,0:T(8,128)S(1)} %fusion.61, f32[2,4,7,2,8,384]{5,4,1,0,2,3:T(8,128)S(1)} %bitcast.341, s32[]{:T(128)S(6)} %select_n.14, f32[7,1,2,384,4,384]{5,4,3,2,1,0:T(4,128)} %get-tuple-element.5), kind=kOutput, calls=%fused_computation.77 | convolution fusion | flops 1585618944 | bytes 34750468 | tf_op jit(solution)/shard_map/efcvr,cfrdq->edcvq/dot_general | solution.py:55
  454.9 25.5 %fusion.103 = f32[2,4,7,1,8,384]{5,4,1,0,2,3:T(8,128)S(1)} fusion(f32[7,2,8,4,384]{4,2,3,1,0:T(8,128)S(1)} %fusion.58, f32[2,4,7,2,8,384]{5,4,1,0,2,3:T(8,128)S(1)} %bitcast.342, s32[]{:T(128)S(6)} %select_n.14, s32[]{:T(128)S(6)} %add.76, f32[7,1,2,384,4,384]{5,4,3,2,1,0:T(4,128)} %get-tuple-element.5), kind=kOutput, calls=%fused_computation.79 | convolution fusion | flops 1585618944 | bytes 34750472 | tf_op jit(solution)/shard_map/efcvr,cfrdq->edcvq/dot_general | solution.py:55
  482.3 46.6 %all-reduce.5.cloned.1.call-done = f32[2,4,7,2,8,384]{5,4,1,0,2,3:T(8,128)} async-done(((f32[2,4,7,2,8,384]{5,4,1,0,2,3:T(8,128)}), f32[2,4,7,2,8,384]{5,4,1,0,2,3:T(8,128)}) %all-reduce.5.cloned.1.call-update) | async-done | bytes 1376272
  528.9 1.8 dynamic-slice_bitcast_fusion.1
  530.8 22.9 %all_to_all.52 = f32[4,7,2,8,384]{4,3,1,2,0:T(8,128)S(1)} all-to-all(f32[4,7,2,8,384]{4,3,1,2,0:T(8,128)S(1)} %copy.99), channel_id=1, replica_groups=mesh['groups'=2,'freq'=4,'src'=2,'vp'=2] {'freq'}, dimensions={0} | all-to-all | bytes 1376256 | tf_op jit(solution)/shard_map/all_to_all | solution.py:85
  553.7 5.1 fusion.157
  558.8 9.1 fusion.42
  568.1 20.5 %all_to_all.53 = f32[4,7,2,8,384]{4,3,2,1,0:T(8,128)} all-to-all(f32[4,7,2,8,384]{4,3,2,1,0:T(8,128)S(1)} %copy.103), channel_id=1, replica_groups=mesh['groups'=2,'freq'=4,'src'=2,'vp'=2] {'freq'}, dimensions={0} | all-to-all | bytes 1376256 | tf_op jit(solution)/shard_map/all_to_all | solution.py:82
  588.7 23.2 %all-gather.13.cloned.1.call-done = f32[8,7,2,8,384]{4,3,2,1,0:T(8,128)} async-done(((f32[4,7,2,8,384]{4,3,2,1,0:T(8,128)}), f32[8,7,2,8,384]{4,3,2,1,0:T(8,128)}) %all-gather.13.cloned.1.call-update) | async-done | bytes 1376272 | tf_op jit(solution)/shard_map/all_gather | solution.py:90
  611.9 1.5 copy.104
  613.4 34.3 %fusion.115 = f32[7,2,8,2,384]{4,2,3,1,0:T(8,128)S(1)} fusion(f32[7,1,2,384,4,384]{5,4,3,2,1,0:T(4,128)} %get-tuple-element.6, f32[2,4,7,2,8,384]{5,4,1,0,2,3:T(8,128)S(1)} %bitcast.331), kind=kOutput, calls=%fused_computation.83 | convolution fusion | flops 1585446912 | bytes 34062336 | tf_op jit(solution)/shard_map/edcvr,cfsdr->efcvs/dot_general | solution.py:41
  647.7 34.3 %fusion.112 = f32[7,2,8,2,384]{4,2,3,1,0:T(8,128)S(1)} fusion(f32[7,1,2,384,4,384]{5,4,3,2,1,0:T(4,128)} %get-tuple-element.6, f32[2,4,7,2,8,384]{5,4,1,0,2,3:T(8,128)S(1)} %bitcast.332), kind=kOutput, calls=%fused_computation.82 | convolution fusion | flops 1585446912 | bytes 34062336 | tf_op jit(solution)/shard_map/edcvr,cfsdr->efcvs/dot_general | solution.py:41
  682.0 34.5 %fusion.133 = f32[2,2,7,1,8,384]{5,4,1,0,2,3:T(8,128)S(1)} fusion(f32[7,2,8,2,384]{4,2,3,1,0:T(8,128)S(1)} %fusion.115, f32[7,1,2,384,4,384]{5,4,3,2,1,0:T(4,128)} %get-tuple-element.5, f32[2,4,7,2,8,384]{5,4,1,0,2,3:T(8,128)S(1)} %bitcast.333), kind=kOutput, calls=%fused_computation.89 | convolution fusion | flops 1585532928 | bytes 34406400 | tf_op jit(solution)/shard_map/edcvr,cfsdr->efcvs/dot_general | solution.py:41
  716.5 34.7 %fusion.139 = f32[2,2,7,1,8,384]{5,4,1,0,2,3:T(8,128)S(1)} fusion(f32[7,2,8,2,384]{4,2,3,1,0:T(8,128)S(1)} %fusion.112, f32[7,1,2,384,4,384]{5,4,3,2,1,0:T(4,128)} %get-tuple-element.5, f32[2,4,7,2,8,384]{5,4,1,0,2,3:T(8,128)S(1)} %bitcast.334), kind=kOutput, calls=%fused_computation.91 | convolution fusion | flops 1585532928 | bytes 34406400 | tf_op jit(solution)/shard_map/edcvr,cfsdr->efcvs/dot_general | solution.py:41
  751.3 12.4 %all_to_all.54 = f32[2,2,7,2,8,384]{5,4,1,2,3,0:T(8,128)S(1)} all-to-all(f32[2,2,7,2,8,384]{5,4,1,2,3,0:T(8,128)S(1)} %copy.105), channel_id=1, replica_groups=mesh['groups'=2,'freq'=4,'src'=2,'vp'=2] {'src'}, dimensions={0} | all-to-all | bytes 1376256 | tf_op jit(solution)/shard_map/all_to_all | solution.py:96
  763.8 21.7 %all_to_all.55 = f32[4,7,2,8,384]{4,3,2,1,0:T(8,128)S(1)} all-to-all(f32[4,7,2,8,384]{4,3,2,1,0:T(8,128)S(1)} %bitcast.350), channel_id=1, replica_groups=mesh['groups'=2,'freq'=4,'src'=2,'vp'=2] {'freq'}, dimensions={0} | all-to-all | bytes 1376256 | tf_op jit(solution)/shard_map/all_to_all | solution.py:85
  785.5 5.2 fusion.155
  790.6 7.0 fusion.40
  797.7 20.1 %all_to_all.56 = f32[4,7,2,8,384]{4,3,2,1,0:T(8,128)} all-to-all(f32[4,7,2,8,384]{4,3,2,1,0:T(8,128)S(1)} %copy.109), channel_id=1, replica_groups=mesh['groups'=2,'freq'=4,'src'=2,'vp'=2] {'freq'}, dimensions={0} | all-to-all | bytes 1376256 | tf_op jit(solution)/shard_map/all_to_all | solution.py:82
  817.9 23.3 %all-gather.15.cloned.1.call-done = f32[8,7,2,8,384]{4,3,2,1,0:T(8,128)} async-done(((f32[4,7,2,8,384]{4,3,2,1,0:T(8,128)}), f32[8,7,2,8,384]{4,3,2,1,0:T(8,128)}) %all-gather.15.cloned.1.call-update) | async-done | bytes 1376272 | tf_op jit(solution)/shard_map/all_gather | solution.py:90
  841.2 1.5 copy.110
  842.6 25.4 %fusion.67 = f32[7,2,8,4,384]{4,2,3,1,0:T(8,128)S(1)} fusion(f32[2,4,7,2,8,384]{5,4,1,0,2,3:T(8,128)S(1)} %bitcast.335, s32[]{:T(128)S(6)} %select_n.14, s32[]{:T(128)S(6)} %add.76, f32[7,1,2,384,4,384]{5,4,3,2,1,0:T(4,128)} %get-tuple-element.6), kind=kOutput, calls=%fused_computation.67 | convolution fusion | flops 1585446912 | bytes 34062344 | tf_op jit(solution)/shard_map/efcvr,cfrdq->edcvq/dot_general | solution.py:55
  868.0 25.4 %fusion.64 = f32[7,2,8,4,384]{4,2,3,1,0:T(8,128)S(1)} fusion(f32[2,4,7,2,8,384]{5,4,1,0,2,3:T(8,128)S(1)} %bitcast.336, s32[]{:T(128)S(6)} %select_n.14, f32[7,1,2,384,4,384]{5,4,3,2,1,0:T(4,128)} %get-tuple-element.6), kind=kOutput, calls=%fused_computation.66 | convolution fusion | flops 1585446912 | bytes 34062340 | tf_op jit(solution)/shard_map/efcvr,cfrdq->edcvq/dot_general | solution.py:55
  893.4 25.7 %fusion.85 = f32[2,4,7,1,8,384]{5,4,1,0,2,3:T(8,128)S(1)} fusion(f32[7,2,8,4,384]{4,2,3,1,0:T(8,128)S(1)} %fusion.67, f32[2,4,7,2,8,384]{5,4,1,0,2,3:T(8,128)S(1)} %bitcast.337, s32[]{:T(128)S(6)} %select_n.14, f32[7,1,2,384,4,384]{5,4,3,2,1,0:T(4,128)} %get-tuple-element.5), kind=kOutput, calls=%fused_computation.73 | convolution fusion | flops 1585618944 | bytes 34750468 | tf_op jit(solution)/shard_map/efcvr,cfrdq->edcvq/dot_general | solution.py:55
  919.1 25.4 %fusion.91 = f32[2,4,7,1,8,384]{5,4,1,0,2,3:T(8,128)S(1)} fusion(f32[7,2,8,4,384]{4,2,3,1,0:T(8,128)S(1)} %fusion.64, f32[2,4,7,2,8,384]{5,4,1,0,2,3:T(8,128)S(1)} %bitcast.338, s32[]{:T(128)S(6)} %select_n.14, s32[]{:T(128)S(6)} %add.76, f32[7,1,2,384,4,384]{5,4,3,2,1,0:T(4,128)} %get-tuple-element.5), kind=kOutput, calls=%fused_computation.75 | convolution fusion | flops 1585618944 | bytes 34750472 | tf_op jit(solution)/shard_map/efcvr,cfrdq->edcvq/dot_general | solution.py:55
  945.7 47.4 %all-reduce.7.cloned.1.call-done = f32[2,4,7,2,8,384]{5,4,1,0,2,3:T(8,128)} async-done(((f32[2,4,7,2,8,384]{5,4,1,0,2,3:T(8,128)}), f32[2,4,7,2,8,384]{5,4,1,0,2,3:T(8,128)}) %all-reduce.7.cloned.1.call-update) | async-done | bytes 1376272
  993.0 1.8 dynamic-slice_bitcast_fusion
  994.9 22.4 %all_to_all.57 = f32[4,7,2,8,384]{4,3,1,2,0:T(8,128)S(1)} all-to-all(f32[4,7,2,8,384]{4,3,1,2,0:T(8,128)S(1)} %copy.115), channel_id=1, replica_groups=mesh['groups'=2,'freq'=4,'src'=2,'vp'=2] {'freq'}, dimensions={0} | all-to-all | bytes 1376256 | tf_op jit(solution)/shard_map/all_to_all | solution.py:85
  1017.4 9.3 select_add_fusion
  (49 shorter events, 12.3 us)
Async XLA Ops:
  20.5 80.9 %all-to-all-start = ((f32[4,7,2,8,384]{4,3,2,1,0:T(8,128)}), f32[4,7,2,8,384]{4,3,2,1,0:T(8,128)S(1)}, u32[]{:S(2)}, u32[]{:S(2)}) async-start(f32[4,7,2,8,384]{4,3,2,1,0:T(8,128)} %copy.84), calls=%async_computation | async-start | bytes 1376256 | tf_op jit(solution)/shard_map/all_to_all | solution.py:82
  26.8 120.1 %all-gather.9.cloned.1.call-start = ((), (), s32[]{:S(2)}) async-start(), calls=%async_computation.10 | async-start | bytes 2064384 | tf_op jit(solution)/shard_map/all_gather | solution.py:90
  101.4 0.8 copy-start
  286.1 39.2 %copy-start.1 = (s32[8,384]{1,0:T(8,128)S(1)}, s32[8,384]{1,0:T(8,128)}, u32[]{:S(2)}) copy-start(s32[8,384]{1,0:T(8,128)} %param.5) | copy-start | bytes 36868
  299.3 20.8 %all-to-all-start.2 = ((f32[4,7,2,8,384]{4,3,2,1,0:T(8,128)}), f32[4,7,2,8,384]{4,3,2,1,0:T(8,128)S(1)}, u32[]{:S(2)}, u32[]{:S(2)}) async-start(f32[4,7,2,8,384]{4,3,2,1,0:T(8,128)} %bitcast.38), calls=%async_computation.2 | async-start | bytes 1376256 | tf_op jit(solution)/shard_map/all_to_all | solution.py:85
  303.3 74.2 %all-gather.11.cloned.1.call-start = ((), (), s32[]{:S(2)}) async-start(), calls=%async_computation.11 | async-start | bytes 2064384 | tf_op jit(solution)/shard_map/all_gather | solution.py:90
  353.0 175.9 %all-reduce.5.cloned.1.call-start = ((), (), s32[]{:S(2)}) async-start(), calls=%async_computation.14 | async-start | bytes 2752512
  454.9 26.8 %copy-start.2 = (u32[32]{0:T(128)S(1)}, u32[32]{0:T(128)}, u32[]{:S(2)}) copy-start(u32[32]{0:T(128)} %constant.39) | copy-start | bytes 388
  481.6 130.3 %all-gather.13.cloned.1.call-start = ((), (), s32[]{:S(2)}) async-start(), calls=%async_computation.12 | async-start | bytes 2064384 | tf_op jit(solution)/shard_map/all_gather | solution.py:90
  588.6 252.5 %all-gather.15.cloned.1.call-start = ((), (), s32[]{:S(2)}) async-start(), calls=%async_computation.13 | async-start | bytes 2064384 | tf_op jit(solution)/shard_map/all_gather | solution.py:90
  817.8 175.2 %all-reduce.7.cloned.1.call-start = ((), (), s32[]{:S(2)}) async-start(), calls=%async_computation.15 | async-start | bytes 2752512
Sparse Core Ops, SparseCore 0:
  102.4 26.4 all-gather.8
  353.1 24.3 all-gather.10
  481.7 47.1 all-reduce.4
  588.8 23.1 all-gather.12
  818.0 23.1 all-gather.14
  945.8 47.1 all-reduce.6
where the time goes:
time: 1040 us; the launch traced here: 1030 us
  matrix products  537 us (52%)
  waiting for transfers between devices  181 us (17%)
  blocking collectives  153 us (15%)
  local copies, waits for them, and re-layouts  133 us (13%)
  between operations  14 us (1%)
  starting transfers between devices  11.5 us (1%)
    dot_general x8, matrix products, product(): jnp.einsum('edcvr,cfsdr->efcvs', left, right, precision=highest_precision)  275 us
    dot_general x8, matrix products, product(): jnp.einsum('efcvr,cfrdq->edcvq', left, right, precision=highest_precision)  203 us
    unnamed x8, waiting for transfers between devices  94.1 us
    reshape x1, local copies, waits for them, and re-layouts, local(): kernel.reshape(slots_here, 2, sub_blocks, traces, freq_count, traces)  74.3 us
    all_gather x4, waiting for transfers between devices, widen(): return lax.all_gather(spectrum[None], 'src', axis=0, tiled=True)  70.5 us
    all_to_all x3, blocking collectives, to_time(): lax.all_to_all(spectrum, 'freq', split_axis=0, concat_axis=0, tiled=True)  67 us
    all_to_all x3, blocking collectives, to_bins(): lax.all_to_all(spectrum, 'freq', split_axis=0, concat_axis=0, tiled=True)  61.2 us
    slice x1, local copies, waits for them, and re-layouts, convolve_pairs(): kernel_view[:, 1]  44.7 us
  transfers between devices with their start and end apart: 8, of which 6 were waited for; matrix products, arithmetic and copies ran while one was open for 12% of the time, Pallas kernels for 0%

commit v1 on v0

--- a/solution.py
+++ b/solution.py
@@ -3,12 +3,18 @@
 import jax
 import jax.numpy as jnp
 from jax import lax
+from jax.experimental import pallas as pl
+from jax.experimental.pallas import tpu as pltpu
 from jax.sharding import PartitionSpec as P
 
 NT = 512
 NF = 24
 FIRST_BIN = 4
 ITERS = 2
+PARTS = 2
+F32 = jnp.float32
+BF16 = jnp.bfloat16
+LIMIT = 56 << 20
 
 
 highest_precision = lax.Precision.HIGHEST
@@ -63,7 +69,7 @@
     return jnp.stack([real_out, imag_out], axis=3)
 
 
-def local(first_field, onset, kernel, bin_owner):
+def local_general(first_field, onset, kernel, bin_owner):
     slots_here = kernel.shape[0]
     freq_count = lax.axis_size("freq")
     src_count = lax.axis_size("src")
@@ -107,6 +113,385 @@
     return focusing
 
 
+def split(x):
+    high = x.astype(BF16)
+    return high, (x - high.astype(F32)).astype(BF16)
+
+
+def stacked_split(x):
+    high, low = split(x)
+    return jnp.concatenate([high.astype(F32), low.astype(F32)], axis=0).astype(BF16)
+
+
+def dot_nt(a, b):
+    return lax.dot_general(a, b, (((1,), (1,)), ((), ())), preferred_element_type=F32)
+
+
+def dot_nn(a, b):
+    return lax.dot_general(a, b, (((1,), (0,)), ((), ())), preferred_element_type=F32)
+
+
+def dot_tn(a, b):
+    return lax.dot_general(a, b, (((0,), (0,)), ((), ())), preferred_element_type=F32)
+
+
+def three_products(dot, both, k):
+    high, low = split(k)
+    rows = both.shape[0] // 2
+    p = dot(both, high)
+    return p[:rows] + p[rows:] + dot(both[:rows], low)
+
+
+def tables(bin_owner, me, slots, freqs):
+    owner = jnp.bitwise_xor(me, jnp.arange(freqs, dtype=jnp.int32))
+    start = jnp.sum((bin_owner[None, :] < owner[:, None]).astype(jnp.int32), axis=1)
+    count = jnp.sum((bin_owner[None, :] == owner[:, None]).astype(jnp.int32), axis=1)
+    slot = jnp.arange(slots, dtype=jnp.int32)
+    index = start[:, None] + slot[None, :] + FIRST_BIN
+    valid = slot[None, :] < count[:, None]
+    sample = jnp.arange(NT, dtype=jnp.int32)
+    phase = index[:, :, None] * sample % NT
+    angle = phase.astype(F32) * (2.0 * math.pi / NT)
+    pair = jnp.stack([jnp.cos(angle), -jnp.sin(angle)], axis=2)
+    return jnp.where(valid[:, :, None, None], pair, 0.0).reshape(freqs * slots * 2, NT)
+
+
+def whole(shape):
+    zeros = (0,) * len(shape)
+    return pl.BlockSpec(shape, lambda *_: zeros)
+
+
+def spectrum_kernel(points, parts, u, table, *rest):
+    outs, scratch, both = rest[:-2], rest[-2], rest[-1]
+    v = pl.program_id(0)
+
+    @pl.when(v == 0)
+    def _():
+        both[...] = stacked_split(table[...])
+
+    rows = table.shape[0]
+    high, low = split(u[0])
+    p = dot_nt(both[...], high)
+    s = p[:rows] + p[rows:] + dot_nt(table[...].astype(BF16), low)
+    set_point(scratch, v, points, s)
+
+    @pl.when(v == points - 1)
+    def _():
+        put_pieces(scratch, outs, points, parts)
+
+
+def set_point(scratch, v, points, value):
+    for i in range(scratch.shape[0]):
+        scratch[i, pl.ds(v, value.shape[0], stride=points), :] = value[:, 128 * i : 128 * i + 128]
+
+
+def get_point(scratch, v, points):
+    tiles = range(scratch.shape[0])
+    rows = scratch.shape[1] // points
+    return jnp.concatenate([scratch[i, pl.ds(v, rows, stride=points), :] for i in tiles], axis=1)
+
+
+def rows_scratch(rows, traces):
+    return pltpu.VMEM((traces // 128, rows, 128), F32)
+
+
+def put_pieces(scratch, outs, points, parts, extra=None):
+    height = 2 * points
+    row = 0
+    slots = sum(parts)
+    for k in range(4):
+        done = 0
+        for n, size in enumerate(parts):
+            for j in range(size):
+                row = (k * slots + done + j) * height
+                for i in range(scratch.shape[0]):
+                    lanes = slice(128 * i, 128 * i + 128)
+                    value = scratch[i, row : row + height, :]
+                    if extra is not None:
+                        value = value + extra[4 * n + k][j, :, lanes]
+                    outs[4 * n + k][j, :, lanes] = value
+            done += size
+
+
+def take_pieces(scratch, ins, points, parts):
+    height = 2 * points
+    slots = sum(parts)
+    for k in range(4):
+        done = 0
+        for n, size in enumerate(parts):
+            for j in range(size):
+                row = (k * slots + done + j) * height
+                for i in range(scratch.shape[0]):
+                    lanes = slice(128 * i, 128 * i + 128)
+                    scratch[i, row : row + height, :] = ins[4 * n + k][j, :, lanes]
+            done += size
+
+
+def piece_shapes(parts, height, traces):
+    return [jax.ShapeDtypeStruct((size, height, traces), F32) for size in parts for _ in range(4)]
+
+
+def spectrum(field, table, parts):
+    points, traces, _ = field.shape
+    rows = table.shape[0]
+    shapes = piece_shapes(parts, 2 * points, traces)
+
+    def kernel(*refs):
+        spectrum_kernel(points, parts, *refs)
+
+    return pl.pallas_call(
+        kernel,
+        grid=(points,),
+        in_specs=[pl.BlockSpec((1, traces, NT), lambda v: (v, 0, 0)), whole(table.shape)],
+        out_specs=[whole(s.shape) for s in shapes],
+        out_shape=shapes,
+        scratch_shapes=[rows_scratch(rows * points, traces), pltpu.VMEM((2 * rows, NT), BF16)],
+        compiler_params=pltpu.CompilerParams(vmem_limit_bytes=LIMIT),
+    )(field, table)
+
+
+def inverse_factor(table, axis):
+    high, low = split(table * (2.0 / NT))
+    third = table.shape[axis] // 3
+    at = lax.broadcasted_iota(jnp.int32, table.shape, axis)
+    middle = (at >= third) & (at < 2 * third)
+    return jnp.where(middle, low.astype(F32), high.astype(F32)).astype(BF16)
+
+
+def field_factor(x):
+    high, low = split(x)
+    high, low = high.astype(F32), low.astype(F32)
+    return jnp.concatenate([high, high, low], axis=0).astype(BF16)
+
+
+def window(pieces, table, onset, parts, extra=None):
+    points, traces = onset.shape
+    rows = table.shape[0]
+    shapes = piece_shapes(parts, 2 * points, traces)
+    count = len(shapes)
+    extra = list(extra) if extra is not None else []
+    backward = jnp.concatenate([table.T] * 3, axis=1)
+
+    def kernel(*refs):
+        ins, refs = refs[:count], refs[count:]
+        more, refs = refs[: len(extra)], refs[len(extra) :]
+        table_ref, back_ref, onset_ref = refs[:3]
+        outs, (x_scratch, y_scratch) = refs[3:-2], refs[-2:]
+        take_pieces(x_scratch, ins, points, parts)
+        forward = stacked_split(table_ref[...])
+        back = inverse_factor(back_ref[...], 1)
+        sample = lax.broadcasted_iota(jnp.int32, (NT, traces), 0)
+        for v in range(points):
+            x = field_factor(get_point(x_scratch, v, points))
+            down = jnp.where(sample < onset_ref[v : v + 1, :], dot_nn(back, x), 0.0)
+            set_point(y_scratch, v, points, transform(forward, table_ref, down))
+        put_pieces(y_scratch, outs, points, parts, more if extra else None)
+
+    def transform(forward, table_ref, down):
+        high, low = split(down)
+        p = dot_nn(forward, high)
+        return p[:rows] + p[rows:] + dot_nn(table_ref[...].astype(BF16), low)
+
+    return pl.pallas_call(
+        kernel,
+        out_shape=shapes,
+        scratch_shapes=[rows_scratch(rows * points, traces)] * 2,
+        compiler_params=pltpu.CompilerParams(vmem_limit_bytes=LIMIT),
+    )(*pieces, *extra, table, backward, onset)
+
+
+def finish(pieces, table, onset, field, parts):
+    points, traces = onset.shape
+    rows = table.shape[0]
+    factor = jnp.concatenate([table] * 3, axis=0)
+    count = len(pieces)
+
+    def kernel(*refs):
+        ins = refs[:count]
+        factor_ref, onset_ref, field_ref, out_ref, scratch = refs[count:]
+        v = pl.program_id(0)
+
+        @pl.when(v == 0)
+        def _():
+            take_pieces(scratch, ins, points, parts)
+
+        x = field_factor(get_point(scratch, v, points))
+        g = dot_tn(x, inverse_factor(factor_ref[...], 0))
+        sample = lax.broadcasted_iota(jnp.int32, (traces, NT), 1)
+        out_ref[0] = field_ref[0] + jnp.where(sample < onset_ref[0], g, 0.0)
+
+    block = pl.BlockSpec((1, traces, NT), lambda v: (v, 0, 0))
+    return pl.pallas_call(
+        kernel,
+        grid=(points,),
+        in_specs=[whole(p.shape) for p in pieces]
+        + [whole(factor.shape), pl.BlockSpec((1, traces, 1), lambda v: (v, 0, 0)), block],
+        out_specs=block,
+        out_shape=jax.ShapeDtypeStruct(field.shape, F32),
+        scratch_shapes=[rows_scratch(rows * points, traces)],
+        compiler_params=pltpu.CompilerParams(vmem_limit_bytes=LIMIT),
+    )(*pieces, factor, onset[:, :, None], field)
+
+
+def put_rows(both, both_turned, at, lanes, piece, sign):
+    half = piece.shape[0] // 2
+    rows = both.shape[0] // 2
+    re, im = piece[:half], piece[half:]
+    turned = jnp.concatenate([-im, re] if sign > 0 else [im, -re], axis=0)
+    for target, value in ((both, piece), (both_turned, turned)):
+        high, low = split(value)
+        target[pl.ds(at, 2 * half), lanes] = high
+        target[pl.ds(pl.multiple_of(rows + at, 16), 2 * half), lanes] = low
+
+
+def convolve(partners, kernel, place, offset):
+    _, slots, height, traces = partners[0].shape
+    quarter = kernel.shape[2] // 2
+    line = kernel.shape[3]
+
+    def body(place_ref, a, b, c, d, k, *rest):
+        outs, (both, turned, g) = rest[:4], rest[4:]
+        me = place_ref[0]
+        for i in range(4):
+            lanes = pl.ds(pl.multiple_of((me ^ i) * traces, 128), traces)
+            for p, ref in enumerate((a, b, c, d)):
+                put_rows(both, turned, p * height, lanes, ref[i, 0], 1)
+        g[...] = three_products(dot_nt, both[...], k[0, 0])
+        g[...] += three_products(dot_nt, turned[...], k[0, 1])
+        for i in range(4):
+            outs[i][0] = g[pl.ds(pl.multiple_of((me ^ i) * height, 16), height), :]
+
+    shape = jax.ShapeDtypeStruct((slots, height, quarter), F32)
+    return pl.pallas_call(
+        body,
+        grid_spec=pltpu.PrefetchScalarGridSpec(
+            num_scalar_prefetch=1,
+            grid=(slots,),
+            in_specs=[pl.BlockSpec((4, 1, height, traces), lambda j, s: (0, j, 0, 0))] * 4
+            + [pl.BlockSpec((1, 2, quarter, line), lambda j, s: (j + offset, 0, s[1], 0))],
+            out_specs=[pl.BlockSpec((1, height, quarter), lambda j, s: (j, 0, 0))] * 4,
+            scratch_shapes=[
+                pltpu.VMEM((8 * height, line), BF16),
+                pltpu.VMEM((8 * height, line), BF16),
+                pltpu.VMEM((4 * height, quarter), F32),
+            ],
+        ),
+        out_shape=[shape] * 4,
+        compiler_params=pltpu.CompilerParams(vmem_limit_bytes=LIMIT),
+    )(place, *partners, kernel)
+
+
+def correlate(pieces, kernel, place, offset, traces):
+    slots, height, quarter = pieces[0].shape
+    line = kernel.shape[3]
+
+    def body(place_ref, a, b, c, d, k, own, other, sibling, both, turned, h):
+        me = place_ref[0]
+        for i, ref in enumerate((a, b, c, d)):
+            at = pl.multiple_of((me ^ i) * height, 16)
+            put_rows(both, turned, at, slice(None), ref[0], -1)
+        h[...] = three_products(dot_nn, both[...], k[0, 0])
+        h[...] += three_products(dot_nn, turned[...], k[0, 1])
+        for i in range(4):
+            lanes = pl.ds(pl.multiple_of((me ^ i) * traces, 128), traces)
+            own[i, 0] = h[:height, lanes]
+            other[i, 0] = h[height : 2 * height, lanes]
+            sibling[0, i, 0] = h[2 * height : 3 * height, lanes]
+            sibling[1, i, 0] = h[3 * height :, lanes]
+
+    one = jax.ShapeDtypeStruct((4, slots, height, traces), F32)
+    two = jax.ShapeDtypeStruct((2, 4, slots, height, traces), F32)
+    one_block = pl.BlockSpec((4, 1, height, traces), lambda j, s: (0, j, 0, 0))
+    two_block = pl.BlockSpec((2, 4, 1, height, traces), lambda j, s: (0, 0, j, 0, 0))
+    return pl.pallas_call(
+        body,
+        grid_spec=pltpu.PrefetchScalarGridSpec(
+            num_scalar_prefetch=1,
+            grid=(slots,),
+            in_specs=[pl.BlockSpec((1, height, quarter), lambda j, s: (j, 0, 0))] * 4
+            + [pl.BlockSpec((1, 2, quarter, line), lambda j, s: (j + offset, 0, s[1], 0))],
+            out_specs=[one_block, one_block, two_block],
+            scratch_shapes=[
+                pltpu.VMEM((8 * height, quarter), BF16),
+                pltpu.VMEM((8 * height, quarter), BF16),
+                pltpu.VMEM((4 * height, line), F32),
+            ],
+        ),
+        out_shape=[one, one, two],
+        compiler_params=pltpu.CompilerParams(vmem_limit_bytes=LIMIT),
+    )(place, *pieces, kernel)
+
+
+def exchange(pieces):
+    out = [pieces[0]]
+    for k in range(1, 4):
+        out.append(lax.ppermute(pieces[k], "freq", [(f, f ^ k) for f in range(4)]))
+    return out
+
+
+def swap(x, axis):
+    return lax.ppermute(x, axis, [(0, 1), (1, 0)])
+
+
+def local_kernels(first_field, onset, kernel, bin_owner):
+    slots = kernel.shape[0]
+    traces = first_field.shape[1]
+    parts = [slots // PARTS + (n < slots % PARTS) for n in range(PARTS)]
+    offsets = [sum(parts[:n]) for n in range(PARTS)]
+    me = lax.axis_index("freq").astype(jnp.int32)
+    core = lax.axis_index("vp").astype(jnp.int32)
+    place = jnp.stack([me, core])
+    table = tables(bin_owner, me, slots, 4)
+    moves = []
+    for f in range(4):
+        for x in range(2):
+            for c in range(2):
+                source = ((2 * x + c) * 2 + (x ^ (f & 1))) * 2 + (c ^ (f >> 1))
+                moves.append((source, (f * 2 + x) * 2 + c))
+    onset_inner = lax.ppermute(onset, ("freq", "src", "vp"), moves)
+
+    def part_of(pieces, n):
+        return pieces[4 * n : 4 * n + 4]
+
+    def conv_part(pieces, n):
+        own = jnp.stack(exchange(pieces))
+        other = swap(own, "src")
+        sibling = swap(own, "vp")
+        across = swap(other, "vp")
+        return convolve((own, other, sibling, across), kernel, place, offsets[n])
+
+    def corr_part(pieces, n):
+        own, other, sibling = correlate(exchange(pieces), kernel, place, offsets[n], traces)
+        from_sibling = swap(sibling, "vp")
+        from_other = swap(other + from_sibling[1], "src")
+        total = own + from_sibling[0] + from_other
+        return exchange([total[k] for k in range(4)])
+
+    first = spectrum(first_field, table, parts)
+    pieces = first
+    for sweep in range(ITERS):
+        out = []
+        for n in range(PARTS):
+            out += exchange(conv_part(part_of(pieces, n), n))
+        inner = window(out, table, onset_inner, parts)
+        out = []
+        for n in range(PARTS):
+            out += corr_part(part_of(inner, n), n)
+        if sweep < ITERS - 1:
+            pieces = window(out, table, onset, parts, first)
+    return finish(out, table, onset, first_field, parts)
+
+
+def local(first_field, onset, kernel, bin_owner):
+    points, traces, samples = first_field.shape
+    quarter = kernel.shape[2] // lax.axis_size("vp")
+    sizes = tuple(lax.axis_size(name) for name in ("freq", "src", "vp"))
+    fits = sizes == (4, 2, 2) and points == 8 and samples == NT
+    if fits and traces % 128 == 0 and quarter == traces and kernel.shape[3] == 4 * traces:
+        return local_kernels(first_field, onset, kernel, bin_owner)
+    return local_general(first_field, onset, kernel, bin_owner)
+
+
 def solution(mesh):
     in_specs = (
         P(("groups", "src", "vp"), "freq", None),

time: 1040 us -> 320 us (0.31)
  matrix products: 537 us -> 0 us
  blocking collectives: 153 us -> 0 us
  local copies, waits for them, and re-layouts: 133 us -> 15.5 us
  Pallas kernels: 0 us -> 115 us
  waiting for transfers between devices: 181 us -> 79.7 us
  starting transfers between devices: 11.5 us -> 96.6 us
  between operations: 14 us -> 0.66 us
    dot_general x26 -> x0, matrix products: 537 us -> none  [the longest x8 275 us: product(): jnp.einsum('edcvr,cfsdr->efcvs', left, right, precision=highest_precision)]
    all_to_all x8 -> x0, blocking collectives: 153 us -> none  [the longest x3 67 us: to_time(): lax.all_to_all(spectrum, 'freq', split_axis=0, concat_axis=0, tiled=True)]
    pallas_call x0 -> x13, Pallas kernels: none -> 115 us  [the longest x4 41.8 us: convolve(): pl.pallas_call(body, grid_spec=pltpu.PrefetchScalarGridSpec(num_scalar_pr...]
    ppermute x0 -> x69, starting transfers between devices: none -> 96.6 us  [the longest x48 85.1 us: exchange(): out.append(lax.ppermute(pieces[k], 'freq', [(f, f ^ k) for f in range(4)]))]
    unnamed x8 -> x0, waiting for transfers between devices: 94.1 us -> none
    ppermute x0 -> x69, waiting for transfers between devices: none -> 79.7 us  [the longest x48 46.1 us: exchange(): out.append(lax.ppermute(pieces[k], 'freq', [(f, f ^ k) for f in range(4)]))]
    reshape x7 -> x0, local copies, waits for them, and re-layouts: 78.2 us -> none  [the longest x1 74.3 us: local(): kernel.reshape(slots_here, 2, sub_blocks, traces, freq_count, traces)]
    all_gather x4 -> x0, waiting for transfers between devices: 70.5 us -> none  [widen(): return lax.all_gather(spectrum[None], 'src', axis=0, tiled=True)]
  transfers between devices with their start and end apart: 8 -> 69, of which waited for: 6 -> 23; matrix products, arithmetic and copies ran while one was open for 12% -> 5% of each run, Pallas kernels for 0% -> 25%
where the time goes in v1:
time: 320 us; the launch traced here: 319 us
  Pallas kernels  115 us (36%)
  starting transfers between devices  96.6 us (30%)
  waiting for transfers between devices  79.7 us (25%)
  local copies, waits for them, and re-layouts  15.5 us (5%)
  other arithmetic  11.7 us (4%)
    ppermute x48, starting transfers between devices, exchange(): out.append(lax.ppermute(pieces[k], 'freq', [(f, f ^ k) for f in range(4)]))  85.1 us
    ppermute x48, waiting for transfers between devices, exchange(): out.append(lax.ppermute(pieces[k], 'freq', [(f, f ^ k) for f in range(4)]))  46.1 us
    pallas_call x4, Pallas kernels, convolve(): pl.pallas_call(body, grid_spec=pltpu.PrefetchScalarGridSpec(num_scalar_pr...  41.8 us
    pallas_call x4, Pallas kernels, correlate(): pl.pallas_call(body, grid_spec=pltpu.PrefetchScalarGridSpec(num_scalar_pr...  39.4 us
    ppermute x20, waiting for transfers between devices, swap(): return lax.ppermute(x, axis, [(0, 1), (1, 0)])  33.6 us
    pallas_call x3, Pallas kernels, window(): pl.pallas_call(kernel, out_shape=shapes, scratch_shapes=[rows_scratch(row...  16.9 us
    ppermute x20, starting transfers between devices, swap(): return lax.ppermute(x, axis, [(0, 1), (1, 0)])  10.8 us
    unnamed x124, local copies, waits for them, and re-layouts  9.82 us
  transfers between devices with their start and end apart: 69, of which 23 were waited for; matrix products, arithmetic and copies ran while one was open for 5% of the time, Pallas kernels for 25%

profile of v1, /device:TPU:0, one launch (start us, length us, event | category | flops | bytes accessed | tf_op | source)
XLA Modules:
  0.0 319.2 jit_solution(11612461969304693328)
XLA Ops:
  2.6 7.6 %shard_map.46 = (f32[4,16,384]{2,1,0:T(8,128)}, f32[4,16,384]{2,1,0:T(8,128)}, f32[4,16,384]{2,1,0:T(8,128)}, f32[4,16,384]{2,1,0:T(8,128)}, f32[3,16,384]{2,1,0...) custom-call(f32[8,384,512]{2,1,0:T(8,128)} %refs_10_.1, ...), custom_call_target="tpu_custom_call" | custom-call | tf_op jit(solution)/shard_map/pallas_call | solution.py:242
  10.2 3.0 collective-permute-start.9
  13.2 2.6 collective-permute-start.10
  16.7 3.5 %collective-permute-start.1 = (f32[4,16,384]{2,1,0:T(8,128)}, f32[4,16,384]{2,1,0:T(8,128)S(1)}, u32[]{:S(2)}, u32[]{:S(2)}) collective-permute-start(f32[4,16,384]{2,1,0:T(8,128)} %get-tuple-element.67.refs_10_), channel_id=1, source_target_pairs={{0,8},{4,12},{8,0},{12,4},{1,9},{5,13},{9,1},{13,5},{2,10},{6,14},... | collective-permute-start | bytes 294920 | tf_op jit(solution)/shard_map/ppermute | solution.py:428
  21.3 1.8 collective-permute-done.11
  25.6 4.4 %collective-permute-done.1 = f32[4,16,384]{2,1,0:T(8,128)S(1)} collective-permute-done((f32[4,16,384]{2,1,0:T(8,128)}, f32[4,16,384]{2,1,0:T(8,128)S(1)}, u32[]{:S(2)}, u32[]{:S(2)}) %collective-permute-start.1) | collective-permute-done | bytes 98336 | tf_op jit(solution)/shard_map/ppermute | solution.py:428
  33.1 7.3 %collective-permute-done.3.b = f32[4,4,16,384]{3,2,1,0:T(8,128)S(1)} collective-permute-done((f32[4,4,16,384]{3,2,1,0:T(8,128)S(1)}, f32[4,4,16,384]{3,2,1,0:T(8,128)S(1)}, u32[]{:S(2)}, u32[]{:S(2)}) %collective-permute-start.3) | collective-permute-done | bytes 393248 | tf_op jit(solution)/shard_map/ppermute | solution.py:433
  43.1 9.6 %shard_map.48 = (f32[3,16,384]{2,1,0:T(8,128)}, f32[3,16,384]{2,1,0:T(8,128)}, f32[3,16,384]{2,1,0:T(8,128)}, f32[3,16,384]{2,1,0:T(8,128)}) custom-call(s32[2]{0:T(128)} %pad_add_fusion.place_ref, f32[4,3,16,384]{3,2,1,0:T(8,128)} %copy-done.3, f32[4,3,16,384]{3,2,1,0:T(8,128)} %copy-done.11, f32[4,3,16,384]{3,2,1,0:T(8,128)} %copy-done.12, ...), custom_call_target="tpu_custom_call" | custom-call | tf_op jit(solution)/shard_map/pallas_call | solution.py:365
  52.7 7.5 %collective-permute-start.15 = (f32[3,16,384]{2,1,0:T(8,128)}, f32[3,16,384]{2,1,0:T(8,128)S(1)}, u32[]{:S(2)}, u32[]{:S(2)}) collective-permute-start(f32[3,16,384]{2,1,0:T(8,128)} %get-tuple-element.78), channel_id=1, source_target_pairs={{0,4},{4,0},{8,12},{12,8},{1,5},{5,1},{9,13},{13,9},{2,6},{6,2},{1... | collective-permute-start | bytes 221192 | tf_op jit(solution)/shard_map/ppermute | solution.py:428
  60.7 1.9 collective-permute-start.17
  63.4 11.3 %shard_map.47 = (f32[4,16,384]{2,1,0:T(8,128)}, f32[4,16,384]{2,1,0:T(8,128)}, f32[4,16,384]{2,1,0:T(8,128)}, f32[4,16,384]{2,1,0:T(8,128)}) custom-call(s32[2]{0:T(128)} %pad_add_fusion.place_ref, f32[4,4,16,384]{3,2,1,0:T(8,128)} %copy-done.1, f32[4,4,16,384]{3,2,1,0:T(8,128)} %copy-done.5, f32[4,4,16,384]{3,2,1,0:T(8,128)} %copy-done.7, ...), custom_call_target="tpu_custom_call" | custom-call | tf_op jit(solution)/shard_map/pallas_call | solution.py:365
  77.3 1.9 collective-permute-start.8
  81.5 5.1 %collective-permute-done.7.refs_2_ = f32[4,16,384]{2,1,0:T(8,128)S(1)} collective-permute-done((f32[4,16,384]{2,1,0:T(8,128)}, f32[4,16,384]{2,1,0:T(8,128)S(1)}, u32[]{:S(2)}, u32[]{:S(2)}) %collective-permute-start.7) | collective-permute-done | bytes 98336 | tf_op jit(solution)/shard_map/ppermute | solution.py:428
  87.3 5.5 %shard_map.49 = (f32[4,16,384]{2,1,0:T(8,128)}, f32[4,16,384]{2,1,0:T(8,128)}, f32[4,16,384]{2,1,0:T(8,128)}, f32[4,16,384]{2,1,0:T(8,128)}, f32[3,16,384]{2,1,0...) custom-call(f32[4,16,384]{2,1,0:T(8,128)} %get-tuple-element.69.refs_0_, ...), custom_call_target="tpu_custom_call" | custom-call | tf_op jit(solution)/shard_map/pallas_call | solution.py:295
  97.9 2.0 collective-permute-start.20
  101.7 1.8 collective-permute-done.28.c
  104.1 9.0 %shard_map.51 = (f32[4,3,16,384]{3,2,1,0:T(8,128)}, f32[4,3,16,384]{3,2,1,0:T(8,128)}, f32[2,4,3,16,384]{4,3,2,1,0:T(8,128)}) custom-call(s32[2]{0:T(128)} %pad_add_fusion.place_ref, f32[3,16,384]{2,1,0:T(8,128)} %get-tuple-element.88.a, f32[3,16,384]{2,1,0:T(8,128)} %copy-done.42, f32[3,16,384]{2,1,0:T(8,128)} %copy-done.44, f32[3,16,384]{2,1,0:T(8,128)} %copy-done.46, ...), custom_call_target="tpu_custom_call" | custom-call | tf_op jit(solution)/shard_map/pallas_call | solution.py:406
  113.8 10.6 %shard_map.50 = (f32[4,4,16,384]{3,2,1,0:T(8,128)}, f32[4,4,16,384]{3,2,1,0:T(8,128)}, f32[2,4,4,16,384]{4,3,2,1,0:T(8,128)}) custom-call(s32[2]{0:T(128)} %pad_add_fusion.place_ref, f32[4,16,384]{2,1,0:T(8,128)} %get-tuple-element.81.a, f32[4,16,384]{2,1,0:T(8,128)} %copy-done.22, f32[4,16,384]{2,1,0:T(8,128)} %copy-done.24, f32[4,16,384]{2,1,0:T(8,128)} %copy-done.27, ...), custom_call_target="tpu_custom_call" | custom-call | tf_op jit(solution)/shard_map/pallas_call | solution.py:406
  129.1 5.9 %collective-permute-done.31 = f32[4,3,16,384]{3,2,1,0:T(8,128)S(1)} collective-permute-done((f32[4,3,16,384]{3,2,1,0:T(8,128)S(1)}, f32[4,3,16,384]{3,2,1,0:T(8,128)S(1)}, u32[]{:S(2)}, u32[]{:S(2)}) %collective-permute-start.31) | collective-permute-done | bytes 294944 | tf_op jit(solution)/shard_map/ppermute | solution.py:433
  135.6 2.1 collective-permute-start.34
  137.8 4.7 %collective-permute-done.23 = f32[4,4,16,384]{3,2,1,0:T(8,128)S(1)} collective-permute-done((f32[4,4,16,384]{3,2,1,0:T(8,128)S(1)}, f32[4,4,16,384]{3,2,1,0:T(8,128)S(1)}, u32[]{:S(2)}, u32[]{:S(2)}) %collective-permute-start.23) | collective-permute-done | bytes 393248 | tf_op jit(solution)/shard_map/ppermute | solution.py:433
  144.2 2.1 collective-permute-start.26
  146.3 4.8 %collective-permute-start.25 = (f32[4,16,384]{2,1,0:T(8,128)S(1)}, f32[4,16,384]{2,1,0:T(8,128)S(1)}, u32[]{:S(2)}, u32[]{:S(2)}) collective-permute-start(f32[4,16,384]{2,1,0:T(8,128)S(1)} %get-tuple-element.132), channel_id=1, source_target_pairs={{0,8},{4,12},{8,0},{12,4},{1,9},{5,13},{9,1},{13,5},{2,10},{6,14},... | collective-permute-start | bytes 294920 | tf_op jit(solution)/shard_map/ppermute | solution.py:428
  151.1 2.4 collective-permute-start.33
  153.5 6.8 %collective-permute-done.33.refs_6_ = f32[3,16,384]{2,1,0:T(8,128)S(1)} collective-permute-done((f32[3,16,384]{2,1,0:T(8,128)S(1)}, f32[3,16,384]{2,1,0:T(8,128)S(1)}, u32[]{:S(2)}, u32[]{:S(2)}) %collective-permute-start.33) | collective-permute-done | bytes 73760 | tf_op jit(solution)/shard_map/ppermute | solution.py:428
  161.1 5.8 %shard_map.52 = (f32[4,16,384]{2,1,0:T(8,128)}, f32[4,16,384]{2,1,0:T(8,128)}, f32[4,16,384]{2,1,0:T(8,128)}, f32[4,16,384]{2,1,0:T(8,128)}, f32[3,16,384]{2,1,0...) custom-call(f32[4,16,384]{2,1,0:T(8,128)} %get-tuple-element.134.refs_0_, ...), custom_call_target="tpu_custom_call" | custom-call | tf_op jit(solution)/shard_map/pallas_call | solution.py:295
  167.0 2.4 collective-permute-start.36
  169.4 2.0 collective-permute-start.37
  171.4 2.4 collective-permute-start.45
  174.7 2.0 collective-permute-start.46
  176.7 2.4 collective-permute-done.36
  184.2 5.0 %collective-permute-done.38.b = f32[4,4,16,384]{3,2,1,0:T(8,128)S(1)} collective-permute-done((f32[4,4,16,384]{3,2,1,0:T(8,128)S(1)}, f32[4,4,16,384]{3,2,1,0:T(8,128)S(1)}, u32[]{:S(2)}, u32[]{:S(2)}) %collective-permute-start.38) | collective-permute-done | bytes 393248 | tf_op jit(solution)/shard_map/ppermute | solution.py:433
  189.7 2.6 collective-permute-done.47.b
  194.7 9.6 %shard_map.54 = (f32[3,16,384]{2,1,0:T(8,128)}, f32[3,16,384]{2,1,0:T(8,128)}, f32[3,16,384]{2,1,0:T(8,128)}, f32[3,16,384]{2,1,0:T(8,128)}) custom-call(s32[2]{0:T(128)} %pad_add_fusion.place_ref, f32[4,3,16,384]{3,2,1,0:T(8,128)} %copy-done.4, f32[4,3,16,384]{3,2,1,0:T(8,128)} %copy-done.14, f32[4,3,16,384]{3,2,1,0:T(8,128)} %copy-done.15, ...), custom_call_target="tpu_custom_call" | custom-call | tf_op jit(solution)/shard_map/pallas_call | solution.py:365
  204.3 3.8 %collective-permute-start.50 = (f32[3,16,384]{2,1,0:T(8,128)}, f32[3,16,384]{2,1,0:T(8,128)S(1)}, u32[]{:S(2)}, u32[]{:S(2)}) collective-permute-start(f32[3,16,384]{2,1,0:T(8,128)} %get-tuple-element.108), channel_id=1, source_target_pairs={{0,4},{4,0},{8,12},{12,8},{1,5},{5,1},{9,13},{13,9},{2,6},{6,2},{1... | collective-permute-start | bytes 221192 | tf_op jit(solution)/shard_map/ppermute | solution.py:428
  209.6 11.3 %shard_map.53 = (f32[4,16,384]{2,1,0:T(8,128)}, f32[4,16,384]{2,1,0:T(8,128)}, f32[4,16,384]{2,1,0:T(8,128)}, f32[4,16,384]{2,1,0:T(8,128)}) custom-call(s32[2]{0:T(128)} %pad_add_fusion.place_ref, f32[4,4,16,384]{3,2,1,0:T(8,128)} %copy-done.2, f32[4,4,16,384]{3,2,1,0:T(8,128)} %copy-done.6, f32[4,4,16,384]{3,2,1,0:T(8,128)} %copy-done.9, ...), custom_call_target="tpu_custom_call" | custom-call | tf_op jit(solution)/shard_map/pallas_call | solution.py:365
  222.2 3.1 collective-permute-start.43
  227.0 11.6 %collective-permute-done.51.refs_6_ = f32[3,16,384]{2,1,0:T(8,128)S(1)} collective-permute-done((f32[3,16,384]{2,1,0:T(8,128)S(1)}, f32[3,16,384]{2,1,0:T(8,128)S(1)}, u32[]{:S(2)}, u32[]{:S(2)}) %collective-permute-start.51) | collective-permute-done | bytes 73760 | tf_op jit(solution)/shard_map/ppermute | solution.py:428
  239.3 5.5 %shard_map.55 = (f32[4,16,384]{2,1,0:T(8,128)}, f32[4,16,384]{2,1,0:T(8,128)}, f32[4,16,384]{2,1,0:T(8,128)}, f32[4,16,384]{2,1,0:T(8,128)}, f32[3,16,384]{2,1,0...) custom-call(f32[4,16,384]{2,1,0:T(8,128)} %get-tuple-element.99.refs_0_, ...), custom_call_target="tpu_custom_call" | custom-call | tf_op jit(solution)/shard_map/pallas_call | solution.py:295
  246.9 2.4 collective-permute-start.63
  251.6 2.1 collective-permute-start.55
  256.1 9.2 %shard_map.57 = (f32[4,3,16,384]{3,2,1,0:T(8,128)}, f32[4,3,16,384]{3,2,1,0:T(8,128)}, f32[2,4,3,16,384]{4,3,2,1,0:T(8,128)}) custom-call(s32[2]{0:T(128)} %pad_add_fusion.place_ref, f32[3,16,384]{2,1,0:T(8,128)} %get-tuple-element.118.a, f32[3,16,384]{2,1,0:T(8,128)} %copy-done.43, f32[3,16,384]{2,1,0:T(8,128)} %copy-done.45, f32[3,16,384]{2,1,0:T(8,128)} %copy-done.47, ...), custom_call_target="tpu_custom_call" | custom-call | tf_op jit(solution)/shard_map/pallas_call | solution.py:406
  266.0 10.6 %shard_map.56 = (f32[4,4,16,384]{3,2,1,0:T(8,128)}, f32[4,4,16,384]{3,2,1,0:T(8,128)}, f32[2,4,4,16,384]{4,3,2,1,0:T(8,128)}) custom-call(s32[2]{0:T(128)} %pad_add_fusion.place_ref, f32[4,16,384]{2,1,0:T(8,128)} %get-tuple-element.111.a, f32[4,16,384]{2,1,0:T(8,128)} %copy-done.21, f32[4,16,384]{2,1,0:T(8,128)} %copy-done.23, f32[4,16,384]{2,1,0:T(8,128)} %copy-done.26, ...), custom_call_target="tpu_custom_call" | custom-call | tf_op jit(solution)/shard_map/pallas_call | solution.py:406
  282.1 5.1 %collective-permute-done.65 = f32[4,3,16,384]{3,2,1,0:T(8,128)S(1)} collective-permute-done((f32[4,3,16,384]{3,2,1,0:T(8,128)S(1)}, f32[4,3,16,384]{3,2,1,0:T(8,128)S(1)}, u32[]{:S(2)}, u32[]{:S(2)}) %collective-permute-start.65) | collective-permute-done | bytes 294944 | tf_op jit(solution)/shard_map/ppermute | solution.py:433
  289.1 5.3 %collective-permute-start.67 = (f32[3,16,384]{2,1,0:T(8,128)S(1)}, f32[3,16,384]{2,1,0:T(8,128)S(1)}, u32[]{:S(2)}, u32[]{:S(2)}) collective-permute-start(f32[3,16,384]{2,1,0:T(8,128)S(1)} %get-tuple-element.136), channel_id=1, source_target_pairs={{0,8},{4,12},{8,0},{12,4},{1,9},{5,13},{9,1},{13,5},{2,10},{6,14},... | collective-permute-start | bytes 221192 | tf_op jit(solution)/shard_map/ppermute | solution.py:428
  298.0 4.9 %collective-permute-start.59 = (f32[4,16,384]{2,1,0:T(8,128)S(1)}, f32[4,16,384]{2,1,0:T(8,128)S(1)}, u32[]{:S(2)}, u32[]{:S(2)}) collective-permute-start(f32[4,16,384]{2,1,0:T(8,128)S(1)} %get-tuple-element.128), channel_id=1, source_target_pairs={{0,8},{4,12},{8,0},{12,4},{1,9},{5,13},{9,1},{13,5},{2,10},{6,14},... | collective-permute-start | bytes 294920 | tf_op jit(solution)/shard_map/ppermute | solution.py:428
  303.7 5.4 %collective-permute-done.59.refs_2_ = f32[4,16,384]{2,1,0:T(8,128)S(1)} collective-permute-done((f32[4,16,384]{2,1,0:T(8,128)S(1)}, f32[4,16,384]{2,1,0:T(8,128)S(1)}, u32[]{:S(2)}, u32[]{:S(2)}) %collective-permute-start.59) | collective-permute-done | bytes 98336 | tf_op jit(solution)/shard_map/ppermute | solution.py:428
  309.8 9.5 %shard_map.58 = f32[8,384,512]{2,1,0:T(8,128)} custom-call(f32[4,16,384]{2,1,0:T(8,128)} %get-tuple-element.130.refs_0_, f32[4,16,384]{2,1,0:T(8,128)} %copy-done.29, f32[4,16,384]{2,1,0:T(8,128)} %copy-done.28, f32[4,16,384]{2,1,0:T(8,128)} %copy-done.25, f32[3,16,384]{2,1,0:T(8,128)} %get-tuple-element.138.refs_4_, f32[3,16,384]{2,1,0:T(8,128)} %copy-done.41, ...), custom_call_target="tpu_custom_call" | custom-call | tf_op jit(solution)/shard_map/pallas_call | solution.py:324
  (260 shorter events, 69.2 us)
Async XLA Ops:
  10.2 10.0 %collective-permute-start.9 = (f32[3,16,384]{2,1,0:T(8,128)}, f32[3,16,384]{2,1,0:T(8,128)S(1)}, u32[]{:S(2)}, u32[]{:S(2)}) collective-permute-start(f32[3,16,384]{2,1,0:T(8,128)} %get-tuple-element.74.refs_13_), channel_id=1, source_target_pairs={{0,4},{4,0},{8,12},{12,8},{1,5},{5,1},{9,13},{13,9},{2,6},{6,2},{1... | collective-permute-start | bytes 221192 | tf_op jit(solution)/shard_map/ppermute | solution.py:428
  15.8 9.8 %collective-permute-start = (f32[4,16,384]{2,1,0:T(8,128)}, f32[4,16,384]{2,1,0:T(8,128)S(1)}, u32[]{:S(2)}, u32[]{:S(2)}) collective-permute-start(f32[4,16,384]{2,1,0:T(8,128)} %get-tuple-element.66.refs_9_), channel_id=1, source_target_pairs={{0,4},{4,0},{8,12},{12,8},{1,5},{5,1},{9,13},{13,9},{2,6},{6,2},{1... | collective-permute-start | bytes 294920 | tf_op jit(solution)/shard_map/ppermute | solution.py:428
  16.7 13.3 %collective-permute-start.1 = (f32[4,16,384]{2,1,0:T(8,128)}, f32[4,16,384]{2,1,0:T(8,128)S(1)}, u32[]{:S(2)}, u32[]{:S(2)}) collective-permute-start(f32[4,16,384]{2,1,0:T(8,128)} %get-tuple-element.67.refs_10_), channel_id=1, source_target_pairs={{0,8},{4,12},{8,0},{12,4},{1,9},{5,13},{9,1},{13,5},{2,10},{6,14},... | collective-permute-start | bytes 294920 | tf_op jit(solution)/shard_map/ppermute | solution.py:428
  20.2 9.8 %collective-permute-start.2 = (f32[4,16,384]{2,1,0:T(8,128)}, f32[4,16,384]{2,1,0:T(8,128)S(1)}, u32[]{:S(2)}, u32[]{:S(2)}) collective-permute-start(f32[4,16,384]{2,1,0:T(8,128)} %get-tuple-element.68.refs_11_), channel_id=1, source_target_pairs={{0,12},{4,8},{8,4},{12,0},{1,13},{5,9},{9,5},{13,1},{2,14},{6,10},... | collective-permute-start | bytes 294920 | tf_op jit(solution)/shard_map/ppermute | solution.py:428
  30.9 9.4 %collective-permute-start.3 = (f32[4,4,16,384]{3,2,1,0:T(8,128)S(1)}, f32[4,4,16,384]{3,2,1,0:T(8,128)S(1)}, u32[]{:S(2)}, u32[]{:S(2)}) collective-permute-start(f32[4,4,16,384]{3,2,1,0:T(8,128)S(1)} %pad_maximum_fusion.a), channel_id=1, source_target_pairs={{0,2},{2,0},{1,3},{3,1},{4,6},{6,4},{5,7},{7,5},{8,10},{10,8},{9,1... | collective-permute-start | bytes 1179656 | tf_op jit(solution)/shard_map/ppermute | solution.py:433
  33.0 27.7 %collective-permute-start.4 = (f32[4,4,16,384]{3,2,1,0:T(8,128)S(1)}, f32[4,4,16,384]{3,2,1,0:T(8,128)S(1)}, u32[]{:S(2)}, u32[]{:S(2)}) collective-permute-start(f32[4,4,16,384]{3,2,1,0:T(8,128)S(1)} %pad_maximum_fusion.a), channel_id=1, source_target_pairs={{0,1},{1,0},{2,3},{3,2},{4,5},{5,4},{6,7},{7,6},{8,9},{9,8},{10,11... | collective-permute-start | bytes 1179656 | tf_op jit(solution)/shard_map/ppermute | solution.py:433
  40.4 22.3 %collective-permute-start.5 = (f32[4,4,16,384]{3,2,1,0:T(8,128)S(1)}, f32[4,4,16,384]{3,2,1,0:T(8,128)S(1)}, u32[]{:S(2)}, u32[]{:S(2)}) collective-permute-start(f32[4,4,16,384]{3,2,1,0:T(8,128)S(1)} %collective-permute-done.3.b), channel_id=1, source_target_pairs={{0,1},{1,0},{2,3},{3,2},{4,5},{5,4},{6,7},{7,6},{8,9},{9,8},{10,11... | collective-permute-start | bytes 1179656 | tf_op jit(solution)/shard_map/ppermute | solution.py:433
  40.4 35.6 %collective-permute-start.18 = (s32[8,384]{1,0:T(8,128)S(1)}, s32[8,384]{1,0:T(8,128)S(1)}, u32[]{:S(2)}, u32[]{:S(2)}) collective-permute-start(s32[8,384]{1,0:T(8,128)S(1)} %copy-done.57), channel_id=1, source_target_pairs={{0,0},{5,1},{10,2},{15,3},{2,4},{7,5},{8,6},{13,7},{1,8},{4,9},{11... | collective-permute-start | bytes 36872 | tf_op jit(solution)/shard_map/ppermute | solution.py:451
  52.7 24.6 %collective-permute-start.15 = (f32[3,16,384]{2,1,0:T(8,128)}, f32[3,16,384]{2,1,0:T(8,128)S(1)}, u32[]{:S(2)}, u32[]{:S(2)}) collective-permute-start(f32[3,16,384]{2,1,0:T(8,128)} %get-tuple-element.78), channel_id=1, source_target_pairs={{0,4},{4,0},{8,12},{12,8},{1,5},{5,1},{9,13},{13,9},{2,6},{6,2},{1... | collective-permute-start | bytes 221192 | tf_op jit(solution)/shard_map/ppermute | solution.py:428
  60.2 20.0 %collective-permute-start.16 = (f32[3,16,384]{2,1,0:T(8,128)}, f32[3,16,384]{2,1,0:T(8,128)S(1)}, u32[]{:S(2)}, u32[]{:S(2)}) collective-permute-start(f32[3,16,384]{2,1,0:T(8,128)} %get-tuple-element.79), channel_id=1, source_target_pairs={{0,8},{4,12},{8,0},{12,4},{1,9},{5,13},{9,1},{13,5},{2,10},{6,14},... | collective-permute-start | bytes 221192 | tf_op jit(solution)/shard_map/ppermute | solution.py:428
  60.7 19.5 %collective-permute-start.17 = (f32[3,16,384]{2,1,0:T(8,128)}, f32[3,16,384]{2,1,0:T(8,128)S(1)}, u32[]{:S(2)}, u32[]{:S(2)}) collective-permute-start(f32[3,16,384]{2,1,0:T(8,128)} %get-tuple-element.80), channel_id=1, source_target_pairs={{0,12},{4,8},{8,4},{12,0},{1,13},{5,9},{9,5},{13,1},{2,14},{6,10},... | collective-permute-start | bytes 221192 | tf_op jit(solution)/shard_map/ppermute | solution.py:428
  75.9 10.7 %collective-permute-start.7 = (f32[4,16,384]{2,1,0:T(8,128)}, f32[4,16,384]{2,1,0:T(8,128)S(1)}, u32[]{:S(2)}, u32[]{:S(2)}) collective-permute-start(f32[4,16,384]{2,1,0:T(8,128)} %get-tuple-element.71), channel_id=1, source_target_pairs={{0,8},{4,12},{8,0},{12,4},{1,9},{5,13},{9,1},{13,5},{2,10},{6,14},... | collective-permute-start | bytes 294920 | tf_op jit(solution)/shard_map/ppermute | solution.py:428
  77.3 9.4 %collective-permute-start.8 = (f32[4,16,384]{2,1,0:T(8,128)}, f32[4,16,384]{2,1,0:T(8,128)S(1)}, u32[]{:S(2)}, u32[]{:S(2)}) collective-permute-start(f32[4,16,384]{2,1,0:T(8,128)} %get-tuple-element.72), channel_id=1, source_target_pairs={{0,12},{4,8},{8,4},{12,0},{1,13},{5,9},{9,5},{13,1},{2,14},{6,10},... | collective-permute-start | bytes 294920 | tf_op jit(solution)/shard_map/ppermute | solution.py:428
  97.3 15.8 %collective-permute-start.19 = (f32[4,16,384]{2,1,0:T(8,128)}, f32[4,16,384]{2,1,0:T(8,128)S(1)}, u32[]{:S(2)}, u32[]{:S(2)}) collective-permute-start(f32[4,16,384]{2,1,0:T(8,128)} %get-tuple-element.82), channel_id=1, source_target_pairs={{0,4},{4,0},{8,12},{12,8},{1,5},{5,1},{9,13},{13,9},{2,6},{6,2},{1... | collective-permute-start | bytes 294920 | tf_op jit(solution)/shard_map/ppermute | solution.py:428
  97.9 15.2 %collective-permute-start.20 = (f32[4,16,384]{2,1,0:T(8,128)}, f32[4,16,384]{2,1,0:T(8,128)S(1)}, u32[]{:S(2)}, u32[]{:S(2)}) collective-permute-start(f32[4,16,384]{2,1,0:T(8,128)} %get-tuple-element.83), channel_id=1, source_target_pairs={{0,8},{4,12},{8,0},{12,4},{1,9},{5,13},{9,1},{13,5},{2,10},{6,14},... | collective-permute-start | bytes 294920 | tf_op jit(solution)/shard_map/ppermute | solution.py:428
  99.9 13.2 %collective-permute-start.21 = (f32[4,16,384]{2,1,0:T(8,128)}, f32[4,16,384]{2,1,0:T(8,128)S(1)}, u32[]{:S(2)}, u32[]{:S(2)}) collective-permute-start(f32[4,16,384]{2,1,0:T(8,128)} %get-tuple-element.84), channel_id=1, source_target_pairs={{0,12},{4,8},{8,4},{12,0},{1,13},{5,9},{9,5},{13,1},{2,14},{6,10},... | collective-permute-start | bytes 294920 | tf_op jit(solution)/shard_map/ppermute | solution.py:428
  113.1 11.9 %collective-permute-start.30 = (f32[2,4,3,16,384]{4,3,2,1,0:T(8,128)}, f32[2,4,3,16,384]{4,3,2,1,0:T(8,128)S(1)}, u32[]{:S(2)}, u32[]{:S(2)}) collective-permute-start(f32[2,4,3,16,384]{4,3,2,1,0:T(8,128)} %get-tuple-element.93), channel_id=1, source_target_pairs={{0,1},{1,0},{2,3},{3,2},{4,5},{5,4},{6,7},{7,6},{8,9},{9,8},{10,11... | collective-permute-start | bytes 1769480 | tf_op jit(solution)/shard_map/ppermute | solution.py:433
  125.0 9.9 %collective-permute-start.31 = (f32[4,3,16,384]{3,2,1,0:T(8,128)S(1)}, f32[4,3,16,384]{3,2,1,0:T(8,128)S(1)}, u32[]{:S(2)}, u32[]{:S(2)}) collective-permute-start(f32[4,3,16,384]{3,2,1,0:T(8,128)S(1)} %fusion.9), channel_id=1, source_target_pairs={{0,2},{2,0},{1,3},{3,1},{4,6},{6,4},{5,7},{7,5},{8,10},{10,8},{9,1... | collective-permute-start | bytes 884744 | tf_op jit(solution)/shard_map/ppermute | solution.py:433
  128.1 14.3 %collective-permute-start.23 = (f32[4,4,16,384]{3,2,1,0:T(8,128)S(1)}, f32[4,4,16,384]{3,2,1,0:T(8,128)S(1)}, u32[]{:S(2)}, u32[]{:S(2)}) collective-permute-start(f32[4,4,16,384]{3,2,1,0:T(8,128)S(1)} %fusion.3), channel_id=1, source_target_pairs={{0,2},{2,0},{1,3},{3,1},{4,6},{6,4},{5,7},{7,5},{8,10},{10,8},{9,1... | collective-permute-start | bytes 1179656 | tf_op jit(solution)/shard_map/ppermute | solution.py:433
  135.6 17.9 %collective-permute-start.34 = (f32[3,16,384]{2,1,0:T(8,128)S(1)}, f32[3,16,384]{2,1,0:T(8,128)S(1)}, u32[]{:S(2)}, u32[]{:S(2)}) collective-permute-start(f32[3,16,384]{2,1,0:T(8,128)S(1)} %get-tuple-element.139), channel_id=1, source_target_pairs={{0,12},{4,8},{8,4},{12,0},{1,13},{5,9},{9,5},{13,1},{2,14},{6,10},... | collective-permute-start | bytes 221192 | tf_op jit(solution)/shard_map/ppermute | solution.py:428
  144.2 16.2 %collective-permute-start.26 = (f32[4,16,384]{2,1,0:T(8,128)S(1)}, f32[4,16,384]{2,1,0:T(8,128)S(1)}, u32[]{:S(2)}, u32[]{:S(2)}) collective-permute-start(f32[4,16,384]{2,1,0:T(8,128)S(1)} %get-tuple-element.131), channel_id=1, source_target_pairs={{0,12},{4,8},{8,4},{12,0},{1,13},{5,9},{9,5},{13,1},{2,14},{6,10},... | collective-permute-start | bytes 294920 | tf_op jit(solution)/shard_map/ppermute | solution.py:428
  146.3 14.1 %collective-permute-start.25 = (f32[4,16,384]{2,1,0:T(8,128)S(1)}, f32[4,16,384]{2,1,0:T(8,128)S(1)}, u32[]{:S(2)}, u32[]{:S(2)}) collective-permute-start(f32[4,16,384]{2,1,0:T(8,128)S(1)} %get-tuple-element.132), channel_id=1, source_target_pairs={{0,8},{4,12},{8,0},{12,4},{1,9},{5,13},{9,1},{13,5},{2,10},{6,14},... | collective-permute-start | bytes 294920 | tf_op jit(solution)/shard_map/ppermute | solution.py:428
  151.1 9.3 %collective-permute-start.24 = (f32[4,16,384]{2,1,0:T(8,128)S(1)}, f32[4,16,384]{2,1,0:T(8,128)S(1)}, u32[]{:S(2)}, u32[]{:S(2)}) collective-permute-start(f32[4,16,384]{2,1,0:T(8,128)S(1)} %get-tuple-element.133), channel_id=1, source_target_pairs={{0,4},{4,0},{8,12},{12,8},{1,5},{5,1},{9,13},{13,9},{2,6},{6,2},{1... | collective-permute-start | bytes 294920 | tf_op jit(solution)/shard_map/ppermute | solution.py:428
  151.1 9.2 %collective-permute-start.33 = (f32[3,16,384]{2,1,0:T(8,128)S(1)}, f32[3,16,384]{2,1,0:T(8,128)S(1)}, u32[]{:S(2)}, u32[]{:S(2)}) collective-permute-start(f32[3,16,384]{2,1,0:T(8,128)S(1)} %get-tuple-element.140), channel_id=1, source_target_pairs={{0,8},{4,12},{8,0},{12,4},{1,9},{5,13},{9,1},{13,5},{2,10},{6,14},... | collective-permute-start | bytes 221192 | tf_op jit(solution)/shard_map/ppermute | solution.py:428
  167.0 12.1 %collective-permute-start.36 = (f32[4,16,384]{2,1,0:T(8,128)}, f32[4,16,384]{2,1,0:T(8,128)S(1)}, u32[]{:S(2)}, u32[]{:S(2)}) collective-permute-start(f32[4,16,384]{2,1,0:T(8,128)} %get-tuple-element.97), channel_id=1, source_target_pairs={{0,8},{4,12},{8,0},{12,4},{1,9},{5,13},{9,1},{13,5},{2,10},{6,14},... | collective-permute-start | bytes 294920 | tf_op jit(solution)/shard_map/ppermute | solution.py:428
  169.4 9.7 %collective-permute-start.37 = (f32[4,16,384]{2,1,0:T(8,128)}, f32[4,16,384]{2,1,0:T(8,128)S(1)}, u32[]{:S(2)}, u32[]{:S(2)}) collective-permute-start(f32[4,16,384]{2,1,0:T(8,128)} %get-tuple-element.98), channel_id=1, source_target_pairs={{0,12},{4,8},{8,4},{12,0},{1,13},{5,9},{9,5},{13,1},{2,14},{6,10},... | collective-permute-start | bytes 294920 | tf_op jit(solution)/shard_map/ppermute | solution.py:428
  171.4 9.3 %collective-permute-start.44 = (f32[3,16,384]{2,1,0:T(8,128)}, f32[3,16,384]{2,1,0:T(8,128)S(1)}, u32[]{:S(2)}, u32[]{:S(2)}) collective-permute-start(f32[3,16,384]{2,1,0:T(8,128)} %get-tuple-element.104), channel_id=1, source_target_pairs={{0,4},{4,0},{8,12},{12,8},{1,5},{5,1},{9,13},{13,9},{2,6},{6,2},{1... | collective-permute-start | bytes 221192 | tf_op jit(solution)/shard_map/ppermute | solution.py:428
  171.4 11.0 %collective-permute-start.45 = (f32[3,16,384]{2,1,0:T(8,128)}, f32[3,16,384]{2,1,0:T(8,128)S(1)}, u32[]{:S(2)}, u32[]{:S(2)}) collective-permute-start(f32[3,16,384]{2,1,0:T(8,128)} %get-tuple-element.105), channel_id=1, source_target_pairs={{0,8},{4,12},{8,0},{12,4},{1,9},{5,13},{9,1},{13,5},{2,10},{6,14},... | collective-permute-start | bytes 221192 | tf_op jit(solution)/shard_map/ppermute | solution.py:428
  180.0 9.2 %collective-permute-start.38 = (f32[4,4,16,384]{3,2,1,0:T(8,128)S(1)}, f32[4,4,16,384]{3,2,1,0:T(8,128)S(1)}, u32[]{:S(2)}, u32[]{:S(2)}) collective-permute-start(f32[4,4,16,384]{3,2,1,0:T(8,128)S(1)} %pad_maximum_fusion.1.a), channel_id=1, source_target_pairs={{0,2},{2,0},{1,3},{3,1},{4,6},{6,4},{5,7},{7,5},{8,10},{10,8},{9,1... | collective-permute-start | bytes 1179656 | tf_op jit(solution)/shard_map/ppermute | solution.py:433
  184.2 23.9 %collective-permute-start.39 = (f32[4,4,16,384]{3,2,1,0:T(8,128)S(1)}, f32[4,4,16,384]{3,2,1,0:T(8,128)S(1)}, u32[]{:S(2)}, u32[]{:S(2)}) collective-permute-start(f32[4,4,16,384]{3,2,1,0:T(8,128)S(1)} %pad_maximum_fusion.1.a), channel_id=1, source_target_pairs={{0,1},{1,0},{2,3},{3,2},{4,5},{5,4},{6,7},{7,6},{8,9},{9,8},{10,11... | collective-permute-start | bytes 1179656 | tf_op jit(solution)/shard_map/ppermute | solution.py:433
  189.2 18.9 %collective-permute-start.40 = (f32[4,4,16,384]{3,2,1,0:T(8,128)S(1)}, f32[4,4,16,384]{3,2,1,0:T(8,128)S(1)}, u32[]{:S(2)}, u32[]{:S(2)}) collective-permute-start(f32[4,4,16,384]{3,2,1,0:T(8,128)S(1)} %collective-permute-done.38.b), channel_id=1, source_target_pairs={{0,1},{1,0},{2,3},{3,2},{4,5},{5,4},{6,7},{7,6},{8,9},{9,8},{10,11... | collective-permute-start | bytes 1179656 | tf_op jit(solution)/shard_map/ppermute | solution.py:433
  204.3 21.1 %collective-permute-start.50 = (f32[3,16,384]{2,1,0:T(8,128)}, f32[3,16,384]{2,1,0:T(8,128)S(1)}, u32[]{:S(2)}, u32[]{:S(2)}) collective-permute-start(f32[3,16,384]{2,1,0:T(8,128)} %get-tuple-element.108), channel_id=1, source_target_pairs={{0,4},{4,0},{8,12},{12,8},{1,5},{5,1},{9,13},{13,9},{2,6},{6,2},{1... | collective-permute-start | bytes 221192 | tf_op jit(solution)/shard_map/ppermute | solution.py:428
  220.9 17.7 %collective-permute-start.41 = (f32[4,16,384]{2,1,0:T(8,128)}, f32[4,16,384]{2,1,0:T(8,128)S(1)}, u32[]{:S(2)}, u32[]{:S(2)}) collective-permute-start(f32[4,16,384]{2,1,0:T(8,128)} %get-tuple-element.100), channel_id=1, source_target_pairs={{0,4},{4,0},{8,12},{12,8},{1,5},{5,1},{9,13},{13,9},{2,6},{6,2},{1... | collective-permute-start | bytes 294920 | tf_op jit(solution)/shard_map/ppermute | solution.py:428
  221.0 17.6 %collective-permute-start.42 = (f32[4,16,384]{2,1,0:T(8,128)}, f32[4,16,384]{2,1,0:T(8,128)S(1)}, u32[]{:S(2)}, u32[]{:S(2)}) collective-permute-start(f32[4,16,384]{2,1,0:T(8,128)} %get-tuple-element.101), channel_id=1, source_target_pairs={{0,8},{4,12},{8,0},{12,4},{1,9},{5,13},{9,1},{13,5},{2,10},{6,14},... | collective-permute-start | bytes 294920 | tf_op jit(solution)/shard_map/ppermute | solution.py:428
  222.2 16.4 %collective-permute-start.43 = (f32[4,16,384]{2,1,0:T(8,128)}, f32[4,16,384]{2,1,0:T(8,128)S(1)}, u32[]{:S(2)}, u32[]{:S(2)}) collective-permute-start(f32[4,16,384]{2,1,0:T(8,128)} %get-tuple-element.102), channel_id=1, source_target_pairs={{0,12},{4,8},{8,4},{12,0},{1,13},{5,9},{9,5},{13,1},{2,14},{6,10},... | collective-permute-start | bytes 294920 | tf_op jit(solution)/shard_map/ppermute | solution.py:428
  225.4 13.2 %collective-permute-start.51 = (f32[3,16,384]{2,1,0:T(8,128)S(1)}, f32[3,16,384]{2,1,0:T(8,128)S(1)}, u32[]{:S(2)}, u32[]{:S(2)}) collective-permute-start(f32[3,16,384]{2,1,0:T(8,128)S(1)} %copy-done.61), channel_id=1, source_target_pairs={{0,8},{4,12},{8,0},{12,4},{1,9},{5,13},{9,1},{13,5},{2,10},{6,14},... | collective-permute-start | bytes 221192 | tf_op jit(solution)/shard_map/ppermute | solution.py:428
  225.4 13.2 %collective-permute-start.52 = (f32[3,16,384]{2,1,0:T(8,128)S(1)}, f32[3,16,384]{2,1,0:T(8,128)S(1)}, u32[]{:S(2)}, u32[]{:S(2)}) collective-permute-start(f32[3,16,384]{2,1,0:T(8,128)S(1)} %copy-done.60), channel_id=1, source_target_pairs={{0,12},{4,8},{8,4},{12,0},{1,13},{5,9},{9,5},{13,1},{2,14},{6,10},... | collective-permute-start | bytes 221192 | tf_op jit(solution)/shard_map/ppermute | solution.py:428
  246.2 9.2 %collective-permute-start.62 = (f32[3,16,384]{2,1,0:T(8,128)}, f32[3,16,384]{2,1,0:T(8,128)S(1)}, u32[]{:S(2)}, u32[]{:S(2)}) collective-permute-start(f32[3,16,384]{2,1,0:T(8,128)} %get-tuple-element.120), channel_id=1, source_target_pairs={{0,8},{4,12},{8,0},{12,4},{1,9},{5,13},{9,1},{13,5},{2,10},{6,14},... | collective-permute-start | bytes 221192 | tf_op jit(solution)/shard_map/ppermute | solution.py:428
  249.3 15.9 %collective-permute-start.53 = (f32[4,16,384]{2,1,0:T(8,128)}, f32[4,16,384]{2,1,0:T(8,128)S(1)}, u32[]{:S(2)}, u32[]{:S(2)}) collective-permute-start(f32[4,16,384]{2,1,0:T(8,128)} %get-tuple-element.112), channel_id=1, source_target_pairs={{0,4},{4,0},{8,12},{12,8},{1,5},{5,1},{9,13},{13,9},{2,6},{6,2},{1... | collective-permute-start | bytes 294920 | tf_op jit(solution)/shard_map/ppermute | solution.py:428
  249.7 15.5 %collective-permute-start.54 = (f32[4,16,384]{2,1,0:T(8,128)}, f32[4,16,384]{2,1,0:T(8,128)S(1)}, u32[]{:S(2)}, u32[]{:S(2)}) collective-permute-start(f32[4,16,384]{2,1,0:T(8,128)} %get-tuple-element.113), channel_id=1, source_target_pairs={{0,8},{4,12},{8,0},{12,4},{1,9},{5,13},{9,1},{13,5},{2,10},{6,14},... | collective-permute-start | bytes 294920 | tf_op jit(solution)/shard_map/ppermute | solution.py:428
  251.6 13.7 %collective-permute-start.55 = (f32[4,16,384]{2,1,0:T(8,128)}, f32[4,16,384]{2,1,0:T(8,128)S(1)}, u32[]{:S(2)}, u32[]{:S(2)}) collective-permute-start(f32[4,16,384]{2,1,0:T(8,128)} %get-tuple-element.114), channel_id=1, source_target_pairs={{0,12},{4,8},{8,4},{12,0},{1,13},{5,9},{9,5},{13,1},{2,14},{6,10},... | collective-permute-start | bytes 294920 | tf_op jit(solution)/shard_map/ppermute | solution.py:428
  265.2 11.9 %collective-permute-start.64 = (f32[2,4,3,16,384]{4,3,2,1,0:T(8,128)}, f32[2,4,3,16,384]{4,3,2,1,0:T(8,128)S(1)}, u32[]{:S(2)}, u32[]{:S(2)}) collective-permute-start(f32[2,4,3,16,384]{4,3,2,1,0:T(8,128)} %get-tuple-element.123), channel_id=1, source_target_pairs={{0,1},{1,0},{2,3},{3,2},{4,5},{5,4},{6,7},{7,6},{8,9},{9,8},{10,11... | collective-permute-start | bytes 1769480 | tf_op jit(solution)/shard_map/ppermute | solution.py:433
  277.2 9.9 %collective-permute-start.65 = (f32[4,3,16,384]{3,2,1,0:T(8,128)S(1)}, f32[4,3,16,384]{3,2,1,0:T(8,128)S(1)}, u32[]{:S(2)}, u32[]{:S(2)}) collective-permute-start(f32[4,3,16,384]{3,2,1,0:T(8,128)S(1)} %fusion.6), channel_id=1, source_target_pairs={{0,2},{2,0},{1,3},{3,1},{4,6},{6,4},{5,7},{7,5},{8,10},{10,8},{9,1... | collective-permute-start | bytes 884744 | tf_op jit(solution)/shard_map/ppermute | solution.py:433
  281.0 13.7 %collective-permute-start.57 = (f32[4,4,16,384]{3,2,1,0:T(8,128)S(1)}, f32[4,4,16,384]{3,2,1,0:T(8,128)S(1)}, u32[]{:S(2)}, u32[]{:S(2)}) collective-permute-start(f32[4,4,16,384]{3,2,1,0:T(8,128)S(1)} %fusion), channel_id=1, source_target_pairs={{0,2},{2,0},{1,3},{3,1},{4,6},{6,4},{5,7},{7,5},{8,10},{10,8},{9,1... | collective-permute-start | bytes 1179656 | tf_op jit(solution)/shard_map/ppermute | solution.py:433
  287.8 15.1 %collective-permute-start.68 = (f32[3,16,384]{2,1,0:T(8,128)S(1)}, f32[3,16,384]{2,1,0:T(8,128)S(1)}, u32[]{:S(2)}, u32[]{:S(2)}) collective-permute-start(f32[3,16,384]{2,1,0:T(8,128)S(1)} %get-tuple-element.135), channel_id=1, source_target_pairs={{0,12},{4,8},{8,4},{12,0},{1,13},{5,9},{9,5},{13,1},{2,14},{6,10},... | collective-permute-start | bytes 221192 | tf_op jit(solution)/shard_map/ppermute | solution.py:428
  289.1 14.6 %collective-permute-start.67 = (f32[3,16,384]{2,1,0:T(8,128)S(1)}, f32[3,16,384]{2,1,0:T(8,128)S(1)}, u32[]{:S(2)}, u32[]{:S(2)}) collective-permute-start(f32[3,16,384]{2,1,0:T(8,128)S(1)} %get-tuple-element.136), channel_id=1, source_target_pairs={{0,8},{4,12},{8,0},{12,4},{1,9},{5,13},{9,1},{13,5},{2,10},{6,14},... | collective-permute-start | bytes 221192 | tf_op jit(solution)/shard_map/ppermute | solution.py:428
  294.4 9.3 %collective-permute-start.66 = (f32[3,16,384]{2,1,0:T(8,128)S(1)}, f32[3,16,384]{2,1,0:T(8,128)S(1)}, u32[]{:S(2)}, u32[]{:S(2)}) collective-permute-start(f32[3,16,384]{2,1,0:T(8,128)S(1)} %get-tuple-element.137), channel_id=1, source_target_pairs={{0,4},{4,0},{8,12},{12,8},{1,5},{5,1},{9,13},{13,9},{2,6},{6,2},{1... | collective-permute-start | bytes 221192 | tf_op jit(solution)/shard_map/ppermute | solution.py:428
  298.0 11.1 %collective-permute-start.59 = (f32[4,16,384]{2,1,0:T(8,128)S(1)}, f32[4,16,384]{2,1,0:T(8,128)S(1)}, u32[]{:S(2)}, u32[]{:S(2)}) collective-permute-start(f32[4,16,384]{2,1,0:T(8,128)S(1)} %get-tuple-element.128), channel_id=1, source_target_pairs={{0,8},{4,12},{8,0},{12,4},{1,9},{5,13},{9,1},{13,5},{2,10},{6,14},... | collective-permute-start | bytes 294920 | tf_op jit(solution)/shard_map/ppermute | solution.py:428
  (83 other events, 553.8 us)
